TPU v7x, 32 devices: a whole 2x2x4 slice. The times are simulated.
32 devices in a mesh: parts: 2 (over x), wide: 8 (over z, y), narrow: 2 (over core).
Axes of the slice: x: 2, y: 2, z: 4, core: 2. Of those that a mesh axis runs over, the one named last changes fastest.
Arguments:
- token_ids: int32 [2048], P('parts'), parts along dimension 0, may hold values from 0 to 128255, as said below
- slab_offset: int32 [2], P('parts'), parts along dimension 0, may hold values from 0 to 26496, as said below
- activations: bfloat16 [2048, 8192], P(('parts', 'wide')), parts along dimension 0, may hold values from -6 to 6
- gate_weight: bfloat16 [8192, 26624], P(None, ('wide', 'narrow')), may hold values from -0.0625 to 0.0625
- up_weight: bfloat16 [8192, 26624], P(None, ('wide', 'narrow')), may hold values from -0.0625 to 0.0625
- prior_slab: float32 [256, 26624], P(('parts', 'narrow'), 'wide'), parts along dimension 0, may hold values from -48 to 48
Outputs:
- new_slab: float32 [256, 26624], P(('parts', 'narrow'), 'wide'), parts along dimension 0
There are 2 independent parts, one for each index of `parts`. A program takes and returns all parts, laid end to end along the dimension named above; an argument that names none is the same for every part. Nothing has to cross between parts.
Inputs may be any that keep to these rules, and one draw needn't show every extreme that they name: `token_ids`: ids at or above 128000 are special tokens. `slab_offset`: A multiple of 64.
All inputs are finite; a program needn't handle non-finite values.
Results may differ from a plain program's by a relative error of at most 0.0039.
Values may be sent and summed in bfloat16 or wider, within the bound.
A program may use at most 192 MiB of HBM per device.

v0:
```python
import jax
import jax.numpy as jnp
from jax import lax
from jax.sharding import PartitionSpec as P

special_first = 128000


def make_keys(features, gate_weight, up_weight):
    gate_sum = jnp.dot(features, gate_weight, preferred_element_type=jnp.float32)
    up_sum = jnp.dot(features, up_weight, preferred_element_type=jnp.float32)
    return (jax.nn.silu(gate_sum) * up_sum).astype(jnp.bfloat16)


def shards(token_ids, slab_offset, activations, gate_weight, up_weight, prior_slab):
    key_rows = make_keys(
        lax.all_gather(activations, "wide", axis=0, tiled=True), gate_weight, up_weight
    )
    columns = lax.all_gather(key_rows, "narrow", axis=1, tiled=True)
    column_count = columns.shape[1]
    row_count = prior_slab.shape[0]
    row_first = slab_offset[0] + lax.axis_index("narrow") * row_count
    holder = row_first // column_count
    inside = row_first % column_count
    candidate = lax.dynamic_slice_in_dim(columns, inside, row_count, 1)
    contribution = jnp.where(
        lax.axis_index("wide") == holder, candidate.astype(jnp.float32), jnp.float32(0.0)
    )
    selected = lax.psum(contribution.astype(jnp.bfloat16), "wide")
    usable = (token_ids < special_first).astype(jnp.bfloat16)[:, None]
    masked = selected * usable
    product = lax.dot_general(
        masked, columns, (((0,), (0,)), ((), ())), preferred_element_type=jnp.float32
    )
    return prior_slab + product


def solution(mesh):
    in_specs = (
        P("parts"),
        P("parts"),
        P(("parts", "wide"), None),
        P(None, ("wide", "narrow")),
        P(None, ("wide", "narrow")),
        P(("parts", "narrow"), "wide"),
    )
    out_specs = P(("parts", "narrow"), "wide")
    return jax.shard_map(shards, mesh=mesh, in_specs=in_specs, out_specs=out_specs, check_vma=False)
```

profile of v0, /device:TPU:0, one launch (start us, length us, event | category | flops | bytes accessed | tf_op | source)
XLA Modules:
  0.0 416.2 jit_solution(253253895124071109)
XLA Ops:
  6.5 0.0 all-gather.3.cloned.1.call-start
  6.5 0.7 all-gather.3.cloned.1.call-update
  7.3 0.0 all-gather.5.cloned.1.call-start
  7.3 232.5 %all-gather.3.cloned.1.call-done = bf16[1024,8192]{1,0:T(8,128)(2,1)} async-done(((bf16[128,8192]{1,0:T(8,128)(2,1)}), bf16[1024,8192]{1,0:T(8,128)(2,1)}) %all-gather.3.cloned.1.call-update) | async-done | bytes 16777232 | tf_op jit(solution)/shard_map/all_gather | solution.py:17
  239.8 0.0 copy-start.2
  239.8 38.1 %fusion.2 = f32[1024,1664]{1,0:T(8,128)} fusion(bf16[1024,8192]{1,0:T(8,128)(2,1)} %all-gather.3.cloned.1.call-done, bf16[8192,1664]{1,0:T(8,128)(2,1)} %param.9), kind=kOutput, calls=%fused_computation.6 | convolution fusion | flops 27917287424 | bytes 50855936 | tf_op jit(solution)/shard_map/dot_general | solution.py:10
  277.9 0.0 copy-done.2
  277.9 0.0 copy-start.1
  277.9 0.0 copy-start
  278.0 35.4 %multiply_convert_fusion = bf16[1024,1664]{1,0:T(8,128)(2,1)} fusion(f32[1024,1664]{1,0:T(8,128)} %fusion.2, bf16[1024,8192]{1,0:T(8,128)(2,1)S(1)} %copy-done.2, bf16[8192,1664]{1,0:T(8,128)(2,1)} %param.10), kind=kOutput, calls=%fused_computation | convolution fusion | flops 27927511040 | bytes 54263808 | tf_op jit(solution)/shard_map/dot_general | solution.py:11
  313.4 0.0 all-gather.5.cloned.1.call-update
  313.4 0.0 all-reduce.2.cloned.1.call-start
  314.1 15.1 %all-gather.5.cloned.1.call-done = bf16[1024,3328]{1,0:T(8,128)(2,1)} async-done(((bf16[1024,1664]{1,0:T(8,128)(2,1)}), bf16[1024,3328]{1,0:T(8,128)(2,1)}) %all-gather.5.cloned.1.call-update) | async-done | bytes 6815760 | tf_op jit(solution)/shard_map/all_gather | solution.py:19
  329.2 1.9 select_convert_fusion
  331.1 0.0 all-reduce.2.cloned.1.call-update
  331.1 0.0 copy-done.1
  331.2 73.2 %all-reduce.2.cloned.1.call-done = bf16[1024,64]{1,0:T(8,128)(2,1)} async-done(((bf16[1024,64]{1,0:T(8,128)(2,1)}), bf16[1024,64]{1,0:T(8,128)(2,1)}) %all-reduce.2.cloned.1.call-update) | async-done | bytes 131088 | tf_op jit(solution)/shard_map/psum | solution.py:29
  404.3 0.0 copy-done
  404.3 5.3 %convolution_add_fusion = f32[64,3328]{1,0:T(8,128)} fusion(f32[64,3328]{1,0:T(8,128)S(1)} %copy-done, bf16[1024,3328]{1,0:T(8,128)(2,1)} %all-gather.5.cloned.1.call-done, bf16[1024,64]{1,0:T(8,128)(2,1)} %all-reduce.2.cloned.1.call-done, bf16[1024]{0:T(1024)(128)(2,1)S(1)} %compare_convert_fusion), kind=kOutput, calls=%fused_computation.1 | convolution fusion | flops 436486144 | bytes 8652800 | tf_op jit(solution)/shard_map/dot_general | solution.py:32
  (1 shorter events, 0.0 us)
Async XLA Ops:
  6.5 233.3 %all-gather.3.cloned.1.call-start = ((), (), s32[]{:S(2)}) async-start(), calls=%async_computation | async-start | bytes 18874368 | tf_op jit(solution)/shard_map/all_gather | solution.py:17
  7.3 322.0 %all-gather.5.cloned.1.call-start = ((), (), s32[]{:S(2)}) async-start(), calls=%async_computation.1 | async-start | bytes 10223616 | tf_op jit(solution)/shard_map/all_gather | solution.py:19
  239.8 38.1 %copy-start.2 = (bf16[1024,8192]{1,0:T(8,128)(2,1)S(1)}, bf16[1024,8192]{1,0:T(8,128)(2,1)}, u32[]{:S(2)}) copy-start(bf16[1024,8192]{1,0:T(8,128)(2,1)} %all-gather.3.cloned.1.call-done) | copy-start | bytes 50331652
  277.9 53.2 %copy-start.1 = (s32[1024]{0:T(1024)S(1)}, s32[1024]{0:T(1024)}, u32[]{:S(2)}) copy-start(s32[1024]{0:T(1024)} %param.6) | copy-start | bytes 12292
  277.9 126.4 %copy-start = (f32[64,3328]{1,0:T(8,128)S(1)}, f32[64,3328]{1,0:T(8,128)}, u32[]{:S(2)}) copy-start(f32[64,3328]{1,0:T(8,128)} %param.11) | copy-start | bytes 2555908
  313.4 90.9 %all-reduce.2.cloned.1.call-start = ((), (), s32[]{:S(2)}) async-start(), calls=%async_computation.2 | async-start | bytes 524288 | tf_op jit(solution)/shard_map/psum | solution.py:29
Sparse Core Ops, SparseCore 0:
  9.5 230.2 all-gather.2
  313.5 15.6 all-gather.4
  332.6 71.7 all-reduce.1
where the time goes:
time: 416 us
  waiting for transfers between devices  322 us (77%)
  matrix products  78.9 us (19%)
  between operations  13.8 us (3%)
    all_gather x1, waiting for transfers between devices, shards(): lax.all_gather(activations, 'wide', axis=0, tiled=True)  233 us
    psum x1, waiting for transfers between devices, shards(): selected = lax.psum(contribution.astype(jnp.bfloat16), 'wide')  73.2 us
    dot_general x1, matrix products, make_keys(): jnp.dot(features, gate_weight, preferred_element_type=jnp.float32)  38.1 us
    dot_general x1, matrix products, make_keys(): up_sum = jnp.dot(features, up_weight, preferred_element_type=jnp.float32)  35.4 us
    all_gather x1, waiting for transfers between devices, shards(): columns = lax.all_gather(key_rows, 'narrow', axis=1, tiled=True)  15.1 us
  transfers between devices with their start and end apart: 3, of which 3 were waited for; matrix products, arithmetic and copies ran while one was open for 0% of the time, Pallas kernels for 0%

commit v1 on v0

--- a/solution.py
+++ b/solution.py
@@ -1,9 +1,16 @@
+import functools
+
 import jax
 import jax.numpy as jnp
 from jax import lax
+from jax.experimental import pallas as pl
+from jax.experimental.pallas import tpu as pltpu
 from jax.sharding import PartitionSpec as P
 
 special_first = 128000
+LINE = 4
+PAIR = 2
+MESH = pl.DeviceIdType.MESH
 
 
 def make_keys(features, gate_weight, up_weight):
@@ -12,7 +19,7 @@
     return (jax.nn.silu(gate_sum) * up_sum).astype(jnp.bfloat16)
 
 
-def shards(token_ids, slab_offset, activations, gate_weight, up_weight, prior_slab):
+def plain_shards(token_ids, slab_offset, activations, gate_weight, up_weight, prior_slab):
     key_rows = make_keys(
         lax.all_gather(activations, "wide", axis=0, tiled=True), gate_weight, up_weight
     )
@@ -35,6 +42,338 @@
     return prior_slab + product
 
 
+def keys_kernel(
+    act, wg, wu, keys, gath, w_v, x_v, k_v,
+    w_sem, x_sem, k_sem, up_send, up_recv, down_send, down_recv, side_send, side_recv,
+    core_send, core_recv,
+):
+    wide = lax.axis_index("wide")
+    core = lax.axis_index("narrow")
+    z, y = wide // PAIR, wide % PAIR
+    rows = act.shape[0]
+    half = rows // 2
+    tiles = w_v.shape[0]
+    up = lax.rem(z + 1, LINE) * PAIR + y
+    down = lax.rem(z + LINE - 1, LINE) * PAIR + y
+    side = z * PAIR + 1 - y
+
+    barrier = pltpu.get_barrier_semaphore()
+    for w in (up, down, side):
+        pl.semaphore_signal(
+            barrier, inc=1, device_id={"wide": w, "narrow": core}, device_id_type=MESH
+        )
+    pl.semaphore_signal(
+        barrier, inc=1, device_id={"wide": wide, "narrow": 1 - core}, device_id_type=MESH
+    )
+
+    def x_copy(src, slot, k):
+        return pltpu.make_async_copy(
+            src, x_v.at[slot, pl.ds(k * rows, rows), :], x_sem.at[slot, k]
+        )
+
+    x_copy(act, 0, 0).start()
+
+    def w_copy(t, k):
+        src = (wg, wu)[k]
+        return pltpu.make_async_copy(
+            src.at[:, pl.ds(pl.multiple_of(t * 128, 128), 128)],
+            w_v.at[t, :, pl.ds(k * 128, 128)],
+            w_sem.at[k, t],
+        )
+
+    @pl.loop(0, tiles)
+    def _(t):
+        w_copy(t, 0).start()
+        w_copy(t, 1).start()
+
+    pl.semaphore_wait(barrier, 4)
+
+    def half_rows(b, c):
+        return pl.ds(pl.multiple_of(b * rows + c * half, 16), half)
+
+    order = (z, z + 1 - 2 * lax.rem(z, 2), 2 - z // 2, 3 - 3 * (z // 2))
+
+    def send(kind, r):
+        block = {"up": z - r, "down": z + r, "side": order[r]}[kind]
+        target = {"up": up, "down": down, "side": side}[kind]
+        ss, rs = {
+            "up": (up_send, up_recv), "down": (down_send, down_recv), "side": (side_send, side_recv)
+        }[kind]
+        b = block * PAIR + y
+        if r == 0:
+            src = act.at[pl.ds(pl.multiple_of(core * half, 16), half), :]
+        else:
+            src = gath.at[half_rows(b, core), :]
+        return pltpu.make_async_remote_copy(
+            src_ref=src, dst_ref=gath.at[half_rows(b, core), :],
+            send_sem=ss.at[r], recv_sem=rs.at[r],
+            device_id={"wide": target, "narrow": core}, device_id_type=MESH,
+        )
+
+    def share(b):
+        part = gath.at[half_rows(b, core), :]
+        return pltpu.make_async_remote_copy(
+            src_ref=part, dst_ref=part, send_sem=core_send.at[b], recv_sem=core_recv.at[b],
+            device_id={"wide": wide, "narrow": 1 - core}, device_id_type=MESH,
+        )
+
+    def sends(kind, r):
+        if kind == "up":
+            return jnp.logical_and(z - r >= 0, z < LINE - 1)
+        return jnp.logical_and(z + r < LINE, z > 0)
+
+    def receives(kind, r):
+        return z - 1 - r >= 0 if kind == "up" else z + 1 + r < LINE
+
+    def push(r):
+        send("side", r).start()
+        if r < LINE - 1:
+            for kind in ("up", "down"):
+                @pl.when(sends(kind, r))
+                def _():
+                    send(kind, r).start()
+
+    def arrive(r):
+        if r < LINE - 1:
+            for kind in ("up", "down"):
+                @pl.when(receives(kind, r))
+                def _():
+                    send(kind, r).wait_recv()
+        send("side", r).wait_recv()
+
+    def spread(r):
+        if r < LINE - 1:
+            for kind in ("up", "down"):
+                @pl.when(receives(kind, r))
+                def _():
+                    block = z - 1 - r if kind == "up" else z + 1 + r
+                    share(block * PAIR + y).start()
+        share(order[r] * PAIR + 1 - y).start()
+
+    def tile(t, count, slot):
+        acc = jnp.dot(x_v[slot, :count, :], w_v[t], preferred_element_type=jnp.float32)
+        g, u = acc[:, :128], acc[:, 128:]
+        k_v[:count, pl.ds(pl.multiple_of(t * 128, 128), 128)] = (
+            g / (1.0 + jnp.exp(-g)) * u
+        ).astype(jnp.bfloat16)
+
+    def k_copy(b, k):
+        return pltpu.make_async_copy(
+            k_v.at[pl.ds(k * rows, rows), :],
+            keys.at[pl.ds(pl.multiple_of(b * rows, 16), rows), :],
+            k_sem.at[k],
+        )
+
+    push(0)
+    x_copy(act, 0, 0).wait()
+
+    @pl.loop(0, tiles)
+    def _(t):
+        w_copy(t, 0).wait()
+        w_copy(t, 1).wait()
+        tile(t, rows, 0)
+
+    done = [k_copy(z * PAIR + y, 0)]
+    done[0].start()
+    for r in range(LINE):
+        arrive(r)
+        if r < LINE - 1:
+            push(r + 1)
+        spread(r)
+        slot = (r + 1) % 2
+        blocks = [order[r] * PAIR + 1 - y]
+        if r < LINE - 1:
+            blocks.append(order[r + 1] * PAIR + y)
+        loads = []
+        for k, b in enumerate(blocks):
+            share(b).wait_recv()
+            load = x_copy(gath.at[pl.ds(pl.multiple_of(b * rows, 16), rows), :], slot, k)
+            load.start()
+            loads.append(load)
+        for load in loads:
+            load.wait()
+        for copy in done:
+            copy.wait()
+
+        @pl.loop(0, tiles)
+        def _(t):
+            tile(t, rows * len(blocks), slot)
+
+        done = [k_copy(b, k) for k, b in enumerate(blocks)]
+        for copy in done:
+            copy.start()
+    for copy in done:
+        copy.wait()
+    for r in range(LINE):
+        send("side", r).wait_send()
+        share(order[r] * PAIR + 1 - y).wait_send()
+        if r:
+            share(order[r] * PAIR + y).wait_send()
+        if r < LINE - 1:
+            for kind in ("up", "down"):
+                @pl.when(sends(kind, r))
+                def _():
+                    send(kind, r).wait_send()
+
+
+def make_key_rows(activations, gate_weight, up_weight):
+    rows, features = activations.shape
+    units = gate_weight.shape[1]
+    tiles = units // 128
+    tokens = rows * LINE * PAIR
+    dma = pltpu.SemaphoreType.DMA
+    return pl.pallas_call(
+        keys_kernel,
+        out_shape=(
+            jax.ShapeDtypeStruct((tokens, units), jnp.bfloat16),
+            jax.ShapeDtypeStruct((tokens, features), jnp.bfloat16),
+        ),
+        in_specs=[pl.BlockSpec(memory_space=pl.ANY)] * 3,
+        out_specs=(pl.BlockSpec(memory_space=pl.ANY),) * 2,
+        scratch_shapes=[
+            pltpu.VMEM((tiles, features, 256), jnp.bfloat16),
+            pltpu.VMEM((2, 2 * rows, features), jnp.bfloat16),
+            pltpu.VMEM((2 * rows, units), jnp.bfloat16),
+            dma((2, tiles)), dma((2, 2)), dma((2,)),
+            dma((LINE - 1,)), dma((LINE - 1,)), dma((LINE - 1,)), dma((LINE - 1,)),
+            dma((LINE,)), dma((LINE,)), dma((LINE * PAIR,)), dma((LINE * PAIR,)),
+        ],
+        compiler_params=pltpu.CompilerParams(
+            collective_id=0, has_side_effects=True, vmem_limit_bytes=63 * 1024 * 1024
+        ),
+        name="gather_keys",
+    )(activations, gate_weight, up_weight)[0]
+
+
+def slab_kernel(
+    group, contribution, usable, keys, prior, out, land, sel, product, other,
+    first_send, first_recv, second_send, second_recv, swap_send, swap_recv,
+):
+    wide = lax.axis_index("wide")
+    core = lax.axis_index("narrow")
+    me = wide * 2 + core
+    span = land.shape[1]
+    row_count = prior.shape[0]
+    units = keys.shape[1]
+
+    def rows_of(g):
+        return pl.ds(pl.multiple_of(g * span, 16), span)
+
+    def device(g):
+        return {"wide": g // 2, "narrow": lax.rem(g, 2)}
+
+    barrier = pltpu.get_barrier_semaphore()
+
+    @pl.loop(1, group)
+    def _(j):
+        pl.semaphore_signal(
+            barrier, inc=1, device_id=device(lax.rem(me + j, group)), device_id_type=MESH
+        )
+
+    pl.semaphore_wait(barrier, group - 1)
+
+    def first(j):
+        target = lax.rem(me + j, group)
+        return pltpu.make_async_remote_copy(
+            src_ref=contribution.at[rows_of(target), :], dst_ref=land.at[j - 1],
+            send_sem=first_send.at[j - 1], recv_sem=first_recv.at[j - 1],
+            device_id=device(target), device_id_type=MESH,
+        )
+
+    def second(j, owner):
+        return pltpu.make_async_remote_copy(
+            src_ref=sel.at[rows_of(owner), :], dst_ref=sel.at[rows_of(owner), :],
+            send_sem=second_send.at[j - 1], recv_sem=second_recv.at[j - 1],
+            device_id=device(lax.rem(me + j, group)), device_id_type=MESH,
+        )
+
+    @pl.loop(1, group)
+    def _(j):
+        first(j).start()
+
+    @pl.loop(1, group)
+    def _(j):
+        first(j).wait_recv()
+
+    total = contribution[rows_of(me), :].astype(jnp.float32)
+    for j in range(1, group):
+        total = total + land[j - 1].astype(jnp.float32)
+    sel[rows_of(me), :] = (total * usable[rows_of(me), :]).astype(jnp.bfloat16)
+
+    @pl.loop(1, group)
+    def _(j):
+        second(j, me).start()
+
+    @pl.loop(1, group)
+    def _(j):
+        second(j, lax.rem(me + group - j, group)).wait_recv()
+
+    product[...] = lax.dot_general(
+        sel[...], keys[...], (((0,), (0,)), ((), ())), preferred_element_type=jnp.float32
+    ).reshape(2, row_count, units)
+
+    swap = pltpu.make_async_remote_copy(
+        src_ref=product.at[1 - core], dst_ref=other,
+        send_sem=swap_send, recv_sem=swap_recv,
+        device_id={"wide": wide, "narrow": 1 - core}, device_id_type=MESH,
+    )
+    swap.start()
+    mine = pl.ds(pl.multiple_of(core * units, 128), units)
+    theirs = pl.ds(pl.multiple_of((1 - core) * units, 128), units)
+    out[:, mine] = prior[:, mine] + product[core]
+    swap.wait_recv()
+    out[:, theirs] = prior[:, theirs] + other[...]
+    swap.wait_send()
+
+    @pl.loop(1, group)
+    def _(j):
+        first(j).wait_send()
+        second(j, me).wait_send()
+
+
+def add_slab(group, contribution, usable, keys, prior):
+    tokens, units = keys.shape
+    row_count, slab_columns = prior.shape
+    span = tokens // group
+    dma = pltpu.SemaphoreType.DMA
+    vmem = pl.BlockSpec(memory_space=pltpu.VMEM)
+    return pl.pallas_call(
+        functools.partial(slab_kernel, group),
+        out_shape=jax.ShapeDtypeStruct(prior.shape, jnp.float32),
+        in_specs=[vmem] * 4,
+        out_specs=vmem,
+        scratch_shapes=[
+            pltpu.VMEM((group - 1, span, 2 * row_count), jnp.bfloat16),
+            pltpu.VMEM((tokens, 2 * row_count), jnp.bfloat16),
+            pltpu.VMEM((2, row_count, units), jnp.float32),
+            pltpu.VMEM((row_count, units), jnp.float32),
+            dma((group - 1,)), dma((group - 1,)), dma((group - 1,)), dma((group - 1,)),
+            dma, dma,
+        ],
+        compiler_params=pltpu.CompilerParams(
+            collective_id=1, has_side_effects=True, vmem_limit_bytes=40 * 1024 * 1024
+        ),
+        name="slab_product",
+    )(contribution, usable, keys, prior)
+
+
+def fused_shards(token_ids, slab_offset, activations, gate_weight, up_weight, prior_slab):
+    keys = make_key_rows(activations, gate_weight, up_weight)
+    units = keys.shape[1]
+    row_count = prior_slab.shape[0]
+    me = lax.axis_index("wide") * 2 + lax.axis_index("narrow")
+    pieces = []
+    for k in range(2):
+        row_first = slab_offset[0] + k * row_count
+        candidate = lax.dynamic_slice_in_dim(keys, row_first % units, row_count, 1)
+        pieces.append(jnp.where(me == row_first // units, candidate, jnp.bfloat16(0.0)))
+    contribution = jnp.concatenate(pieces, axis=1)
+    usable = jnp.broadcast_to(
+        (token_ids < special_first).astype(jnp.float32)[:, None], contribution.shape
+    )
+    return add_slab(LINE * PAIR * 2, contribution, usable, keys, prior_slab)
+
+
 def solution(mesh):
     in_specs = (
         P("parts"),
@@ -45,4 +384,5 @@
         P(("parts", "narrow"), "wide"),
     )
     out_specs = P(("parts", "narrow"), "wide")
+    shards = fused_shards if mesh.shape["wide"] == LINE * PAIR else plain_shards
     return jax.shard_map(shards, mesh=mesh, in_specs=in_specs, out_specs=out_specs, check_vma=False)

time: 416 us -> 142 us (0.34)
  waiting for transfers between devices: 322 us -> 0 us
  Pallas kernels: 0 us -> 136 us
  matrix products: 78.9 us -> 0 us
  between operations: 13.8 us -> 0.79 us
    all_gather x2 -> x0, waiting for transfers between devices: 248 us -> none  [the longest x1 233 us: shards(): lax.all_gather(activations, 'wide', axis=0, tiled=True)]
    pallas_call x0 -> x2, Pallas kernels: none -> 136 us  [the longest x1 118 us: make_key_rows(): pl.pallas_call(keys_kernel, out_shape=(jax.ShapeDtypeStruct((tokens, unit...]
    dot_general x3 -> x0, matrix products: 78.9 us -> none  [the longest x1 38.1 us: make_keys(): jnp.dot(features, gate_weight, preferred_element_type=jnp.float32)]
    psum x1 -> x0, waiting for transfers between devices: 73.2 us -> none  [shards(): selected = lax.psum(contribution.astype(jnp.bfloat16), 'wide')]
  transfers between devices with their start and end apart: 3 -> 0, of which waited for: 3 -> 0; matrix products, arithmetic and copies ran while one was open for 0% -> 0% of each run, Pallas kernels for 0% -> 0%
where the time goes in v1:
time: 142 us
  Pallas kernels  136 us (96%)
  local copies, waits for them, and re-layouts  3.06 us (2%)
  other arithmetic  1.61 us (1%)
    pallas_call x1, Pallas kernels, make_key_rows(): pl.pallas_call(keys_kernel, out_shape=(jax.ShapeDtypeStruct((tokens, unit...  118 us
    pallas_call x1, Pallas kernels, add_slab(): pl.pallas_call(functools.partial(slab_kernel, group), out_shape=jax.Shape...  18.5 us
    unnamed x7, local copies, waits for them, and re-layouts  2.87 us

profile of v1, /device:TPU:0, one launch (start us, length us, event | category | flops | bytes accessed | tf_op | source)
XLA Modules:
  0.0 141.9 jit_solution(666247942171407060)
XLA Ops:
  0.0 0.0 copy-start.2
  0.0 0.0 copy-start.1
  0.0 118.0 %gather_keys.1 = (bf16[1024,1664]{1,0:T(8,128)(2,1)}, bf16[1024,8192]{1,0:T(8,128)(2,1)}) custom-call(bf16[128,8192]{1,0:T(8,128)(2,1)} %act.1, bf16[8192,1664]{1,0:T(8,128)(2,1)} %wg.1, bf16[8192,1664]{1,0:T(8,128)(2,1)} %wu.1), custom_call_target="tpu_custom_call" | custom-call | tf_op jit(solution)/shard_map/gather_keys/pallas_call | solution.py:225
  118.7 1.5 %dynamic-slice_select_fusion.1 = (bf16[1024,64]{1,0:T(8,128)(2,1)S(1)}, bf16[1024,64]{1,0:T(8,128)(2,1)S(1)}) fusion(bf16[1024,1664]{1,0:T(8,128)(2,1)} %get-tuple-element.6.keys, s32[]{:T(128)S(6)} %select_n.41, pred[]{:T(512)S(6)} %eq.9, s32[]{:T(128)S(6)} %select_n.46, pred[]{:T(512)S(6)} %eq.10), kind=kLoop, calls=%fused_computation.2 | loop fusion | flops 131072 | bytes 524298 | tf_op jit(solution)/shard_map/jit(_where)/select_n | solution.py:369
  120.2 0.1 pad_maximum_fusion.contribution
  120.3 0.0 copy-done.2
  120.3 0.2 broadcast_in_dim.12.usable
  120.5 0.0 copy-done.1
  120.5 0.0 copy-start
  120.6 2.0 %copy-done = bf16[1024,1664]{1,0:T(8,128)(2,1)S(1)} copy-done((bf16[1024,1664]{1,0:T(8,128)(2,1)S(1)}, bf16[1024,1664]{1,0:T(8,128)(2,1)}, u32[]{:S(2)}) %copy-start) | copy-done | bytes 3407896
  122.5 18.5 %slab_product.1 = f32[64,3328]{1,0:T(8,128)S(1)} custom-call(bf16[1024,128]{1,0:T(8,128)(2,1)S(1)} %pad_maximum_fusion.contribution, f32[1024,128]{1,0:T(8,128)S(1)} %broadcast_in_dim.12.usable, bf16[1024,1664]{1,0:T(8,128)(2,1)S(1)} %copy-done, f32[64,3328]{1,0:T(8,128)S(1)} %copy-done.1), custom_call_target="tpu_custom_call" | custom-call | tf_op jit(solution)/shard_map/slab_product/pallas_call | solution.py:340
  141.0 0.9 copy.9
  (1 shorter events, 0.0 us)
Async XLA Ops:
  0.0 120.3 %copy-start.2 = (s32[1024]{0:T(1024)S(1)}, s32[1024]{0:T(1024)}, u32[]{:S(2)}) copy-start(s32[1024]{0:T(1024)} %param.6) | copy-start | bytes 12292
  0.0 120.5 %copy-start.1 = (f32[64,3328]{1,0:T(8,128)S(1)}, f32[64,3328]{1,0:T(8,128)}, u32[]{:S(2)}) copy-start(f32[64,3328]{1,0:T(8,128)} %prior.1) | copy-start | bytes 2555908
  120.5 2.0 %copy-start = (bf16[1024,1664]{1,0:T(8,128)(2,1)S(1)}, bf16[1024,1664]{1,0:T(8,128)(2,1)}, u32[]{:S(2)}) copy-start(bf16[1024,1664]{1,0:T(8,128)(2,1)} %get-tuple-element.6.keys) | copy-start | bytes 10223620

commit v2 on v1

--- a/solution.py
+++ b/solution.py
@@ -10,6 +10,7 @@
 special_first = 128000
 LINE = 4
 PAIR = 2
+AHEAD = 4
 MESH = pl.DeviceIdType.MESH
 
 
@@ -45,17 +46,19 @@
 def keys_kernel(
     act, wg, wu, keys, gath, w_v, x_v, k_v,
     w_sem, x_sem, k_sem, up_send, up_recv, down_send, down_recv, side_send, side_recv,
-    core_send, core_recv,
+    core_send, core_recv, cross_send, cross_recv,
 ):
     wide = lax.axis_index("wide")
     core = lax.axis_index("narrow")
     z, y = wide // PAIR, wide % PAIR
     rows = act.shape[0]
-    half = rows // 2
+    piece = rows // 4
     tiles = w_v.shape[0]
+    odd = lax.rem(z, 2)
     up = lax.rem(z + 1, LINE) * PAIR + y
     down = lax.rem(z + LINE - 1, LINE) * PAIR + y
     side = z * PAIR + 1 - y
+    cross = (z + 1 - 2 * odd) * PAIR + y
 
     barrier = pltpu.get_barrier_semaphore()
     for w in (up, down, side):
@@ -66,12 +69,8 @@
         barrier, inc=1, device_id={"wide": wide, "narrow": 1 - core}, device_id_type=MESH
     )
 
-    def x_copy(src, slot, k):
-        return pltpu.make_async_copy(
-            src, x_v.at[slot, pl.ds(k * rows, rows), :], x_sem.at[slot, k]
-        )
-
-    x_copy(act, 0, 0).start()
+    own_load = pltpu.make_async_copy(act, x_v.at[0, pl.ds(0, rows), :], x_sem.at[0, 0])
+    own_load.start()
 
     def w_copy(t, k):
         src = (wg, wu)[k]
@@ -81,39 +80,38 @@
             w_sem.at[k, t],
         )
 
-    @pl.loop(0, tiles)
-    def _(t):
-        w_copy(t, 0).start()
-        w_copy(t, 1).start()
-
     pl.semaphore_wait(barrier, 4)
 
-    def half_rows(b, c):
-        return pl.ds(pl.multiple_of(b * rows + c * half, 16), half)
-
-    order = (z, z + 1 - 2 * lax.rem(z, 2), 2 - z // 2, 3 - 3 * (z // 2))
-
-    def send(kind, r):
-        block = {"up": z - r, "down": z + r, "side": order[r]}[kind]
-        target = {"up": up, "down": down, "side": side}[kind]
-        ss, rs = {
-            "up": (up_send, up_recv), "down": (down_send, down_recv), "side": (side_send, side_recv)
-        }[kind]
-        b = block * PAIR + y
-        if r == 0:
-            src = act.at[pl.ds(pl.multiple_of(core * half, 16), half), :]
+    def rows_of(b, c, s):
+        return pl.ds(pl.multiple_of(b * rows + (c * 2 + s) * piece, 16), piece)
+
+    order = (z, 1 + odd, lax.rem(z + 2, LINE), 3 - 3 * odd)
+
+    def relay(b, s, own, target, ss, rs):
+        if own:
+            src = act.at[pl.ds(pl.multiple_of((core * 2 + s) * piece, 16), piece), :]
         else:
-            src = gath.at[half_rows(b, core), :]
+            src = gath.at[rows_of(b, core, s), :]
         return pltpu.make_async_remote_copy(
-            src_ref=src, dst_ref=gath.at[half_rows(b, core), :],
-            send_sem=ss.at[r], recv_sem=rs.at[r],
+            src_ref=src, dst_ref=gath.at[rows_of(b, core, s), :], send_sem=ss, recv_sem=rs,
             device_id={"wide": target, "narrow": core}, device_id_type=MESH,
         )
 
-    def share(b):
-        part = gath.at[half_rows(b, core), :]
+    def send(kind, r, s):
+        if kind == "up":
+            b, t, ss, rs = (z - r) * PAIR + y, up, up_send, up_recv
+        elif kind == "down":
+            b, t, ss, rs = (z + r) * PAIR + y, down, down_send, down_recv
+        elif kind == "side":
+            b, t, ss, rs = order[r] * PAIR + y, side, side_send, side_recv
+        else:
+            b, t, ss, rs = 3 * odd * PAIR + 1 - y, cross, cross_send, cross_recv
+        return relay(b, s, r == 0, t, ss.at[r, s], rs.at[r, s])
+
+    def share(b, s):
+        part = gath.at[rows_of(b, core, s), :]
         return pltpu.make_async_remote_copy(
-            src_ref=part, dst_ref=part, send_sem=core_send.at[b], recv_sem=core_recv.at[b],
+            src_ref=part, dst_ref=part, send_sem=core_send.at[b, s], recv_sem=core_recv.at[b, s],
             device_id={"wide": wide, "narrow": 1 - core}, device_id_type=MESH,
         )
 
@@ -125,95 +123,162 @@
     def receives(kind, r):
         return z - 1 - r >= 0 if kind == "up" else z + 1 + r < LINE
 
-    def push(r):
-        send("side", r).start()
-        if r < LINE - 1:
-            for kind in ("up", "down"):
-                @pl.when(sends(kind, r))
-                def _():
-                    send(kind, r).start()
-
-    def arrive(r):
-        if r < LINE - 1:
+    def last_kind(s):
+        return ("side", "cross")[s]
+
+    def push(r, s):
+        if r == LINE - 1:
+            send(last_kind(s), r, s).start()
+            return
+        for kind in ("up", "down"):
+            @pl.when(sends(kind, r))
+            def _():
+                send(kind, r, s).start()
+        send("side", r, s).start()
+
+    def arrive(r, s):
+        if r == LINE - 1:
+            send(last_kind(s), r, s).wait_recv()
+        else:
             for kind in ("up", "down"):
                 @pl.when(receives(kind, r))
                 def _():
-                    send(kind, r).wait_recv()
-        send("side", r).wait_recv()
-
-    def spread(r):
-        if r < LINE - 1:
+                    send(kind, r, s).wait_recv()
+            send("side", r, s).wait_recv()
+            push(r + 1, s)
             for kind in ("up", "down"):
                 @pl.when(receives(kind, r))
                 def _():
                     block = z - 1 - r if kind == "up" else z + 1 + r
-                    share(block * PAIR + y).start()
-        share(order[r] * PAIR + 1 - y).start()
-
-    def tile(t, count, slot):
-        acc = jnp.dot(x_v[slot, :count, :], w_v[t], preferred_element_type=jnp.float32)
+                    share(block * PAIR + y, s).start()
+        share(order[r] * PAIR + 1 - y, s).start()
+
+    def tile(t, slot, first, count):
+        acc = jnp.dot(
+            x_v[slot, first:first + count, :], w_v[t], preferred_element_type=jnp.float32
+        )
         g, u = acc[:, :128], acc[:, 128:]
-        k_v[:count, pl.ds(pl.multiple_of(t * 128, 128), 128)] = (
+        k_v[first:first + count, pl.ds(pl.multiple_of(t * 128, 128), 128)] = (
             g / (1.0 + jnp.exp(-g)) * u
         ).astype(jnp.bfloat16)
 
-    def k_copy(b, k):
-        return pltpu.make_async_copy(
-            k_v.at[pl.ds(k * rows, rows), :],
-            keys.at[pl.ds(pl.multiple_of(b * rows, 16), rows), :],
-            k_sem.at[k],
-        )
-
-    push(0)
-    x_copy(act, 0, 0).wait()
-
-    @pl.loop(0, tiles)
-    def _(t):
+    def fetch(blocks, s, slot):
+        loads, spans = [], []
+        for b in blocks:
+            share(b, s).wait_recv()
+            for c in range(2):
+                k = s * 4 + len(spans)
+                spans.append(rows_of(b, c, s))
+                load = pltpu.make_async_copy(
+                    gath.at[spans[-1], :],
+                    x_v.at[slot, pl.ds(k * piece, piece), :],
+                    x_sem.at[slot, k],
+                )
+                load.start()
+                loads.append(load)
+        return loads, spans
+
+    def finish(copies):
+        for copy in copies:
+            copy.wait()
+
+    def store(spans, first):
+        copies = []
+        for k, span in enumerate(spans, first // piece):
+            copies.append(
+                pltpu.make_async_copy(
+                    k_v.at[pl.ds(k * piece, piece), :], keys.at[span, :], k_sem.at[k]
+                )
+            )
+            copies[-1].start()
+        return copies
+
+    def multiply(slot, first, count, start, stop):
+        @pl.loop(start, stop)
+        def _(t):
+            tile(t, slot, first, count)
+
+    def pair(r):
+        return order[r] * PAIR + 1 - y, order[r + 1] * PAIR + y
+
+    for s in range(2):
+        push(0, s)
+    ahead = min(AHEAD, tiles)
+    for t in range(ahead):
+        w_copy(t, 0).start()
+        w_copy(t, 1).start()
+    own_load.wait()
+
+    def first_tile(t):
         w_copy(t, 0).wait()
         w_copy(t, 1).wait()
-        tile(t, rows, 0)
-
-    done = [k_copy(z * PAIR + y, 0)]
-    done[0].start()
-    for r in range(LINE):
-        arrive(r)
-        if r < LINE - 1:
-            push(r + 1)
-        spread(r)
-        slot = (r + 1) % 2
-        blocks = [order[r] * PAIR + 1 - y]
-        if r < LINE - 1:
-            blocks.append(order[r + 1] * PAIR + y)
-        loads = []
-        for k, b in enumerate(blocks):
-            share(b).wait_recv()
-            load = x_copy(gath.at[pl.ds(pl.multiple_of(b * rows, 16), rows), :], slot, k)
+
+        @pl.when(t + ahead < tiles)
+        def _():
+            w_copy(t + ahead, 0).start()
+            w_copy(t + ahead, 1).start()
+
+        tile(t, 0, 0, rows)
+
+    pl.loop(0, tiles // 2)(first_tile)
+    arrive(0, 0)
+    pl.loop(tiles // 2, tiles - 1)(first_tile)
+    loads, spans = fetch(pair(0), 0, 1)
+    arrive(0, 1)
+    pl.loop(tiles - 1, tiles)(first_tile)
+    own_store = store([rows_of(z * PAIR + y, k // 2, k % 2) for k in range(4)], 0)
+    more, rest = fetch(pair(0), 1, 1)
+    finish(loads + more + own_store)
+    early = (9 * tiles) // 13
+    multiply(1, 0, 2 * rows, 0, early)
+    arrive(1, 0)
+    multiply(1, 0, 2 * rows, early, tiles - 1)
+    loads, ahead_spans = fetch(pair(1), 0, 0)
+    multiply(1, 0, 2 * rows, tiles - 1, tiles)
+    stores = store(spans + rest, 0)
+    done = [stores[:4], stores[4:]]
+    spans = ahead_spans
+    last = order[LINE - 1] * PAIR + 1 - y
+    for r, s, at in ((1, 0, 8), (1, 1, 10), (2, 0, 10), (2, 1, 11)):
+        slot, first = r - 1, s * rows
+        finish(loads + done[s])
+        at = (at * tiles) // 13
+        multiply(slot, first, rows, 0, at)
+        if r < LINE - 2 or s == 0:
+            arrive(r + s, 1 - s)
+            multiply(slot, first, rows, at, tiles)
+            done[s] = store(spans, first)
+            loads, spans = fetch(pair(r + s), 1 - s, r + s - 1)
+        else:
+            arrive(r + 1, 0)
+            multiply(slot, first, rows, at, tiles)
+            done[s] = store(spans, first)
+            arrive(r + 1, 1)
+            for t in range(2):
+                share(last, t).wait_recv()
+            load = pltpu.make_async_copy(
+                gath.at[pl.ds(pl.multiple_of(last * rows, 16), rows), :],
+                x_v.at[0, pl.ds(0, rows), :],
+                x_sem.at[0, 0],
+            )
             load.start()
-            loads.append(load)
-        for load in loads:
-            load.wait()
-        for copy in done:
-            copy.wait()
-
-        @pl.loop(0, tiles)
-        def _(t):
-            tile(t, rows * len(blocks), slot)
-
-        done = [k_copy(b, k) for k, b in enumerate(blocks)]
-        for copy in done:
-            copy.start()
-    for copy in done:
-        copy.wait()
-    for r in range(LINE):
-        send("side", r).wait_send()
-        share(order[r] * PAIR + 1 - y).wait_send()
-        if r:
-            share(order[r] * PAIR + y).wait_send()
-        if r < LINE - 1:
-            for kind in ("up", "down"):
-                @pl.when(sends(kind, r))
-                def _():
-                    send(kind, r).wait_send()
+            loads = [load]
+    finish(loads + done[0])
+    multiply(0, 0, rows, 0, tiles)
+    finish(store([rows_of(last, k // 2, k % 2) for k in range(4)], 0) + done[1])
+    for s in range(2):
+        for r in range(LINE):
+            share(order[r] * PAIR + 1 - y, s).wait_send()
+            if r:
+                share(order[r] * PAIR + y, s).wait_send()
+            if r == LINE - 1:
+                send(last_kind(s), r, s).wait_send()
+            else:
+                send("side", r, s).wait_send()
+                for kind in ("up", "down"):
+                    @pl.when(sends(kind, r))
+                    def _():
+                        send(kind, r, s).wait_send()
 
 
 def make_key_rows(activations, gate_weight, up_weight):
@@ -234,9 +299,10 @@
             pltpu.VMEM((tiles, features, 256), jnp.bfloat16),
             pltpu.VMEM((2, 2 * rows, features), jnp.bfloat16),
             pltpu.VMEM((2 * rows, units), jnp.bfloat16),
-            dma((2, tiles)), dma((2, 2)), dma((2,)),
-            dma((LINE - 1,)), dma((LINE - 1,)), dma((LINE - 1,)), dma((LINE - 1,)),
-            dma((LINE,)), dma((LINE,)), dma((LINE * PAIR,)), dma((LINE * PAIR,)),
+            dma((2, tiles)), dma((2, 8)), dma((8,)),
+            dma((LINE, 2)), dma((LINE, 2)), dma((LINE, 2)), dma((LINE, 2)),
+            dma((LINE, 2)), dma((LINE, 2)), dma((LINE * PAIR, 2)), dma((LINE * PAIR, 2)),
+            dma((LINE, 2)), dma((LINE, 2)),
         ],
         compiler_params=pltpu.CompilerParams(
             collective_id=0, has_side_effects=True, vmem_limit_bytes=63 * 1024 * 1024
@@ -246,9 +312,16 @@
 
 
 def slab_kernel(
-    group, contribution, usable, keys, prior, out, land, sel, product, other,
+    group, contribution, usable, keys_hbm, prior_hbm, out, keys, prior, load_sem, land, sel,
+    product, other,
     first_send, first_recv, second_send, second_recv, swap_send, swap_recv,
 ):
+    loads = [
+        pltpu.make_async_copy(keys_hbm, keys, load_sem.at[0]),
+        pltpu.make_async_copy(prior_hbm, prior, load_sem.at[1]),
+    ]
+    for load in loads:
+        load.start()
     wide = lax.axis_index("wide")
     core = lax.axis_index("narrow")
     me = wide * 2 + core
@@ -308,6 +381,8 @@
     def _(j):
         second(j, lax.rem(me + group - j, group)).wait_recv()
 
+    for load in loads:
+        load.wait()
     product[...] = lax.dot_general(
         sel[...], keys[...], (((0,), (0,)), ((), ())), preferred_element_type=jnp.float32
     ).reshape(2, row_count, units)
@@ -340,9 +415,12 @@
     return pl.pallas_call(
         functools.partial(slab_kernel, group),
         out_shape=jax.ShapeDtypeStruct(prior.shape, jnp.float32),
-        in_specs=[vmem] * 4,
+        in_specs=[vmem] * 2 + [pl.BlockSpec(memory_space=pl.ANY)] * 2,
         out_specs=vmem,
         scratch_shapes=[
+            pltpu.VMEM(keys.shape, jnp.bfloat16),
+            pltpu.VMEM(prior.shape, jnp.float32),
+            dma((2,)),
             pltpu.VMEM((group - 1, span, 2 * row_count), jnp.bfloat16),
             pltpu.VMEM((tokens, 2 * row_count), jnp.bfloat16),
             pltpu.VMEM((2, row_count, units), jnp.float32),

time: 142 us -> 137 us (0.965)
  Pallas kernels: 136 us -> 131 us
    pallas_call x1, Pallas kernels: 118 us -> 112 us  [make_key_rows(): pl.pallas_call(keys_kernel, out_shape=(jax.ShapeDtypeStruct((tokens, unit...]
where the time goes in v2:
time: 137 us; the launch traced here: 136 us
  Pallas kernels  131 us (96%)
  local copies, waits for them, and re-layouts  3.06 us (2%)
  other arithmetic  1.61 us (1%)
    pallas_call x1, Pallas kernels, make_key_rows(): pl.pallas_call(keys_kernel, out_shape=(jax.ShapeDtypeStruct((tokens, unit...  112 us
    pallas_call x1, Pallas kernels, add_slab(): pl.pallas_call(functools.partial(slab_kernel, group), out_shape=jax.Shape...  18.3 us
    unnamed x7, local copies, waits for them, and re-layouts  2.87 us

profile of v2, /device:TPU:0, one launch (start us, length us, event | category | flops | bytes accessed | tf_op | source)
XLA Modules:
  0.0 136.2 jit_solution(12302118118216543661)
XLA Ops:
  0.0 0.0 copy-start.2
  0.0 0.0 copy-start.1
  0.0 112.4 %gather_keys.1 = (bf16[1024,1664]{1,0:T(8,128)(2,1)}, bf16[1024,8192]{1,0:T(8,128)(2,1)}) custom-call(bf16[128,8192]{1,0:T(8,128)(2,1)} %act.1, bf16[8192,1664]{1,0:T(8,128)(2,1)} %wg.1, bf16[8192,1664]{1,0:T(8,128)(2,1)} %wu.1), custom_call_target="tpu_custom_call" | custom-call | tf_op jit(solution)/shard_map/gather_keys/pallas_call | solution.py:290
  113.2 1.5 %dynamic-slice_select_fusion.1 = (bf16[1024,64]{1,0:T(8,128)(2,1)S(1)}, bf16[1024,64]{1,0:T(8,128)(2,1)S(1)}) fusion(bf16[1024,1664]{1,0:T(8,128)(2,1)} %get-tuple-element.6.keys_hbm, s32[]{:T(128)S(6)} %select_n.41, pred[]{:T(512)S(6)} %eq.9, s32[]{:T(128)S(6)} %select_n.46, pred[]{:T(512)S(6)} %eq.10), kind=kLoop, calls=%fused_computation.2 | loop fusion | flops 131072 | bytes 524298 | tf_op jit(solution)/shard_map/jit(_where)/select_n | solution.py:447
  114.6 0.1 pad_maximum_fusion.contribution
  114.8 0.0 copy-done.2
  114.8 0.2 broadcast_in_dim.12.usable
  115.0 0.0 copy-done.1
  115.0 0.0 copy-start
  115.0 2.0 %copy-done = bf16[1024,1664]{1,0:T(8,128)(2,1)S(1)} copy-done((bf16[1024,1664]{1,0:T(8,128)(2,1)S(1)}, bf16[1024,1664]{1,0:T(8,128)(2,1)}, u32[]{:S(2)}) %copy-start) | copy-done | bytes 3407896
  117.0 18.3 %slab_product.1 = f32[64,3328]{1,0:T(8,128)S(1)} custom-call(bf16[1024,128]{1,0:T(8,128)(2,1)S(1)} %pad_maximum_fusion.contribution, f32[1024,128]{1,0:T(8,128)S(1)} %broadcast_in_dim.12.usable, bf16[1024,1664]{1,0:T(8,128)(2,1)S(1)} %copy-done, f32[64,3328]{1,0:T(8,128)S(1)} %copy-done.1), custom_call_target="tpu_custom_call" | custom-call | tf_op jit(solution)/shard_map/slab_product/pallas_call | solution.py:415
  135.3 0.9 copy.9
  (1 shorter events, 0.0 us)
Async XLA Ops:
  0.0 114.8 %copy-start.2 = (s32[1024]{0:T(1024)S(1)}, s32[1024]{0:T(1024)}, u32[]{:S(2)}) copy-start(s32[1024]{0:T(1024)} %param.6) | copy-start | bytes 12292
  0.0 115.0 %copy-start.1 = (f32[64,3328]{1,0:T(8,128)S(1)}, f32[64,3328]{1,0:T(8,128)}, u32[]{:S(2)}) copy-start(f32[64,3328]{1,0:T(8,128)} %prior_hbm.1) | copy-start | bytes 2555908
  115.0 2.0 %copy-start = (bf16[1024,1664]{1,0:T(8,128)(2,1)S(1)}, bf16[1024,1664]{1,0:T(8,128)(2,1)}, u32[]{:S(2)}) copy-start(bf16[1024,1664]{1,0:T(8,128)(2,1)} %get-tuple-element.6.keys_hbm) | copy-start | bytes 10223620

commit v3 on v2

--- a/solution.py
+++ b/solution.py
@@ -313,7 +313,7 @@
 
 def slab_kernel(
     group, contribution, usable, keys_hbm, prior_hbm, out, keys, prior, load_sem, land, sel,
-    product, other,
+    product, other, mix, twin_half, twin_send, twin_recv,
     first_send, first_recv, second_send, second_recv, swap_send, swap_recv,
 ):
     loads = [
@@ -324,41 +324,55 @@
         load.start()
     wide = lax.axis_index("wide")
     core = lax.axis_index("narrow")
-    me = wide * 2 + core
     span = land.shape[1]
+    half = mix.shape[0]
     row_count = prior.shape[0]
     units = keys.shape[1]
-
-    def rows_of(g):
-        return pl.ds(pl.multiple_of(g * span, 16), span)
-
-    def device(g):
-        return {"wide": g // 2, "narrow": lax.rem(g, 2)}
+    twin = {"wide": wide, "narrow": 1 - core}
+
+    def peer(j):
+        return {"wide": lax.rem(wide + j, group), "narrow": core}
+
+    def half_of(c):
+        return pl.ds(pl.multiple_of(c * half, 16), half)
+
+    def rows_of(w):
+        return pl.ds(pl.multiple_of(w * span, 16), span)
+
+    def slice_of(w):
+        return pl.ds(pl.multiple_of(core * half + w * span, 16), span)
 
     barrier = pltpu.get_barrier_semaphore()
 
     @pl.loop(1, group)
     def _(j):
-        pl.semaphore_signal(
-            barrier, inc=1, device_id=device(lax.rem(me + j, group)), device_id_type=MESH
-        )
-
-    pl.semaphore_wait(barrier, group - 1)
+        pl.semaphore_signal(barrier, inc=1, device_id=peer(j), device_id_type=MESH)
+
+    pl.semaphore_signal(barrier, inc=1, device_id=twin, device_id_type=MESH)
+    pl.semaphore_wait(barrier, group)
 
     def first(j):
-        target = lax.rem(me + j, group)
         return pltpu.make_async_remote_copy(
-            src_ref=contribution.at[rows_of(target), :], dst_ref=land.at[j - 1],
+            src_ref=mix.at[rows_of(lax.rem(wide + j, group)), :], dst_ref=land.at[j - 1],
             send_sem=first_send.at[j - 1], recv_sem=first_recv.at[j - 1],
-            device_id=device(target), device_id_type=MESH,
+            device_id=peer(j), device_id_type=MESH,
         )
 
     def second(j, owner):
         return pltpu.make_async_remote_copy(
-            src_ref=sel.at[rows_of(owner), :], dst_ref=sel.at[rows_of(owner), :],
+            src_ref=sel.at[slice_of(owner), :], dst_ref=sel.at[slice_of(owner), :],
             send_sem=second_send.at[j - 1], recv_sem=second_recv.at[j - 1],
-            device_id=device(lax.rem(me + j, group)), device_id_type=MESH,
-        )
+            device_id=peer(j), device_id_type=MESH,
+        )
+
+    merge = pltpu.make_async_remote_copy(
+        src_ref=contribution.at[half_of(1 - core), :], dst_ref=twin_half,
+        send_sem=twin_send.at[0], recv_sem=twin_recv.at[0],
+        device_id=twin, device_id_type=MESH,
+    )
+    merge.start()
+    merge.wait_recv()
+    mix[...] = contribution[half_of(core), :] + twin_half[...]
 
     @pl.loop(1, group)
     def _(j):
@@ -368,19 +382,26 @@
     def _(j):
         first(j).wait_recv()
 
-    total = contribution[rows_of(me), :].astype(jnp.float32)
+    total = mix[rows_of(wide), :].astype(jnp.float32)
     for j in range(1, group):
         total = total + land[j - 1].astype(jnp.float32)
-    sel[rows_of(me), :] = (total * usable[rows_of(me), :]).astype(jnp.bfloat16)
-
-    @pl.loop(1, group)
-    def _(j):
-        second(j, me).start()
-
-    @pl.loop(1, group)
-    def _(j):
-        second(j, lax.rem(me + group - j, group)).wait_recv()
-
+    sel[slice_of(wide), :] = (total * usable[slice_of(wide), :]).astype(jnp.bfloat16)
+
+    @pl.loop(1, group)
+    def _(j):
+        second(j, wide).start()
+
+    @pl.loop(1, group)
+    def _(j):
+        second(j, lax.rem(wide + group - j, group)).wait_recv()
+
+    spread = pltpu.make_async_remote_copy(
+        src_ref=sel.at[half_of(core), :], dst_ref=sel.at[half_of(core), :],
+        send_sem=twin_send.at[1], recv_sem=twin_recv.at[1],
+        device_id=twin, device_id_type=MESH,
+    )
+    spread.start()
+    spread.wait_recv()
     for load in loads:
         load.wait()
     product[...] = lax.dot_general(
@@ -403,13 +424,16 @@
     @pl.loop(1, group)
     def _(j):
         first(j).wait_send()
-        second(j, me).wait_send()
+        second(j, wide).wait_send()
+
+    merge.wait_send()
+    spread.wait_send()
 
 
 def add_slab(group, contribution, usable, keys, prior):
     tokens, units = keys.shape
     row_count, slab_columns = prior.shape
-    span = tokens // group
+    span = tokens // (2 * group)
     dma = pltpu.SemaphoreType.DMA
     vmem = pl.BlockSpec(memory_space=pltpu.VMEM)
     return pl.pallas_call(
@@ -425,6 +449,9 @@
             pltpu.VMEM((tokens, 2 * row_count), jnp.bfloat16),
             pltpu.VMEM((2, row_count, units), jnp.float32),
             pltpu.VMEM((row_count, units), jnp.float32),
+            pltpu.VMEM((tokens // 2, 2 * row_count), jnp.bfloat16),
+            pltpu.VMEM((tokens // 2, 2 * row_count), jnp.bfloat16),
+            dma((2,)), dma((2,)),
             dma((group - 1,)), dma((group - 1,)), dma((group - 1,)), dma((group - 1,)),
             dma, dma,
         ],
@@ -449,7 +476,7 @@
     usable = jnp.broadcast_to(
         (token_ids < special_first).astype(jnp.float32)[:, None], contribution.shape
     )
-    return add_slab(LINE * PAIR * 2, contribution, usable, keys, prior_slab)
+    return add_slab(LINE * PAIR, contribution, usable, keys, prior_slab)
 
 
 def solution(mesh):

time: 137 us -> 135 us (0.985)
  Pallas kernels: 131 us -> 129 us
    pallas_call x1, Pallas kernels: 18.3 us -> 16.5 us  [add_slab(): pl.pallas_call(functools.partial(slab_kernel, group), out_shape=jax.Shape...]
where the time goes in v3:
time: 135 us; the launch traced here: 134 us
  Pallas kernels  129 us (96%)
  local copies, waits for them, and re-layouts  3.06 us (2%)
  other arithmetic  1.68 us (1%)
    pallas_call x1, Pallas kernels, make_key_rows(): pl.pallas_call(keys_kernel, out_shape=(jax.ShapeDtypeStruct((tokens, unit...  112 us
    pallas_call x1, Pallas kernels, add_slab(): pl.pallas_call(functools.partial(slab_kernel, group), out_shape=jax.Shape...  16.5 us
    unnamed x7, local copies, waits for them, and re-layouts  2.87 us

profile of v3, /device:TPU:0, one launch (start us, length us, event | category | flops | bytes accessed | tf_op | source)
XLA Modules:
  0.0 134.5 jit_solution(16086114349842375915)
XLA Ops:
  0.0 0.0 copy-start.2
  0.0 0.0 copy-start.1
  0.0 112.4 %gather_keys.1 = (bf16[1024,1664]{1,0:T(8,128)(2,1)}, bf16[1024,8192]{1,0:T(8,128)(2,1)}) custom-call(bf16[128,8192]{1,0:T(8,128)(2,1)} %act.1, bf16[8192,1664]{1,0:T(8,128)(2,1)} %wg.1, bf16[8192,1664]{1,0:T(8,128)(2,1)} %wu.1), custom_call_target="tpu_custom_call" | custom-call | tf_op jit(solution)/shard_map/gather_keys/pallas_call | solution.py:290
  113.2 1.5 %dynamic-slice_select_fusion.1 = (bf16[1024,64]{1,0:T(8,128)(2,1)S(1)}, bf16[1024,64]{1,0:T(8,128)(2,1)S(1)}) fusion(bf16[1024,1664]{1,0:T(8,128)(2,1)} %get-tuple-element.6.keys_hbm, s32[]{:T(128)S(6)} %select_n.41, pred[]{:T(512)S(6)} %eq.9, s32[]{:T(128)S(6)} %select_n.46, pred[]{:T(512)S(6)} %eq.10), kind=kLoop, calls=%fused_computation.2 | loop fusion | flops 131072 | bytes 524298 | tf_op jit(solution)/shard_map/jit(_where)/select_n | solution.py:474
  114.7 0.1 pad_maximum_fusion.contribution
  114.9 0.0 copy-done.2
  114.9 0.2 broadcast_in_dim.12.usable
  115.1 0.0 copy-done.1
  115.1 0.0 copy-start
  115.1 2.0 %copy-done = bf16[1024,1664]{1,0:T(8,128)(2,1)S(1)} copy-done((bf16[1024,1664]{1,0:T(8,128)(2,1)S(1)}, bf16[1024,1664]{1,0:T(8,128)(2,1)}, u32[]{:S(2)}) %copy-start) | copy-done | bytes 3407896
  117.1 16.5 %slab_product.1 = f32[64,3328]{1,0:T(8,128)S(1)} custom-call(bf16[1024,128]{1,0:T(8,128)(2,1)S(1)} %pad_maximum_fusion.contribution, f32[1024,128]{1,0:T(8,128)S(1)} %broadcast_in_dim.12.usable, bf16[1024,1664]{1,0:T(8,128)(2,1)S(1)} %copy-done, f32[64,3328]{1,0:T(8,128)S(1)} %copy-done.1), custom_call_target="tpu_custom_call" | custom-call | tf_op jit(solution)/shard_map/slab_product/pallas_call | solution.py:439
  133.6 0.9 copy.9
  (1 shorter events, 0.0 us)
Async XLA Ops:
  0.0 114.9 %copy-start.2 = (s32[1024]{0:T(1024)S(1)}, s32[1024]{0:T(1024)}, u32[]{:S(2)}) copy-start(s32[1024]{0:T(1024)} %param.6) | copy-start | bytes 12292
  0.0 115.1 %copy-start.1 = (f32[64,3328]{1,0:T(8,128)S(1)}, f32[64,3328]{1,0:T(8,128)}, u32[]{:S(2)}) copy-start(f32[64,3328]{1,0:T(8,128)} %prior_hbm.1) | copy-start | bytes 2555908
  115.1 2.0 %copy-start = (bf16[1024,1664]{1,0:T(8,128)(2,1)S(1)}, bf16[1024,1664]{1,0:T(8,128)(2,1)}, u32[]{:S(2)}) copy-start(bf16[1024,1664]{1,0:T(8,128)(2,1)} %get-tuple-element.6.keys_hbm) | copy-start | bytes 10223620
